TPU v7x, 512 devices: a whole 4x4x16 slice. The times are simulated.
512 devices in a mesh: lat: 16 (over x_hi, y, core), lon: 32 (over x_lo, z).
Axes of the slice: x: 4 (x_hi: 2, x_lo: 2; x = x_hi * 2 + x_lo), y: 4, z: 16, core: 2. Of those that a mesh axis runs over, the one named last changes fastest.
Arguments:
- adjoint_in: float32 [64, 256, 8192], P(None, 'lat', 'lon'), may hold values from -6 to 6
- u_courant: float32 [64, 256, 1024], P('lon', 'lat'), may hold values from -0.24 to 0.24
- v_courant: float32 [64, 256, 1024], P('lon', 'lat'), may hold values from -0.24 to 0.24
- diffusivity: float32 [64, 256, 1024], P('lon', 'lat'), may hold values from 0.025 to 1000
- surface_factor: float32 [256, 8192], P('lat', 'lon'), may hold values from 0.3 to 3
- zonal_sqrt: float32 [1024, 1024], P(None, 'lon'), may hold values from 0 to 1, as said below
Outputs:
- adjoint_out: float32 [64, 256, 8192], P(None, 'lat', 'lon')
- flux_gradient: float32 [256, 8192], P('lat', 'lon')
Inputs may be any that keep to these rules, and one draw needn't show every extreme that they name: zonal_sqrt is symmetric and positive.
All inputs are finite; a program needn't handle non-finite values.
Results may differ from a plain program's by a relative error of at most 0.00013.
Values sent between devices are 32-bit elements; how exact they have to be, the bound alone decides.
A program may use at most 64 MiB of HBM per device.

v0:
```python
import jax
import jax.numpy as jnp
from jax import lax
from jax.experimental import pallas as pl
from jax.experimental.pallas import tpu as pltpu
from jax.sharding import PartitionSpec as P

MESH = pl.DeviceIdType.MESH
F32 = jnp.float32
NSUB = 4
TRAC = 8
NLA = 16
NLO = 32
NZ = 16
HALF = 8
LAG = 2
CH = 4
PER = 2
LOOK = 4
NG = 8


def lon_of(slot):
    group = slot // 4
    return lax.rem(group, 2) * NZ + (group // 2) * 4 + lax.rem(slot, 4)


def slot_of(lon):
    z = lax.rem(lon, NZ)
    return 8 * (z // 4) + 4 * (lon // NZ) + lax.rem(z, 4)


def iota(axis):
    return lax.broadcasted_iota(jnp.int32, (8, 128), axis)


def lroll(value, shift):
    shift = shift % 128
    return value if shift == 0 else pltpu.roll(value, shift, 1)


def sroll(value, shift):
    shift = shift % 8
    return value if shift == 0 else pltpu.roll(value, shift, 0)


def lanes_of(value, index):
    return jnp.take_along_axis(value, index, axis=1, mode="promise_in_bounds")


def quarters(values, base):
    quarter = iota(1) // 32
    result = lroll(values[0], base)
    for q in range(1, 4):
        result = jnp.where(quarter == q, lroll(values[q], base + 32 * q), result)
    return result


def rows16(slot):
    return pl.ds(pl.multiple_of(16 * slot, 16), 16)


def pack_slabs(u_v, v_v, k_v, uv_out, ek_out, top):
    lane, sub = iota(1), iota(0)
    part = lax.rem(lane, 32) // 4

    def group(g, carry):
        def tile(ref, level, half, at):
            value = ref[level, 8 * half : 8 * half + 8, pl.ds(pl.multiple_of(at * 128, 128), 128)]
            if ref is v_v and half == 1:
                value = jnp.where(jnp.logical_and(top, sub == 7), 0.0, value)
            return value

        after, before = lax.rem(g + 1, 8), lax.rem(g + 7, 8)
        rims = []
        for level in range(2):
            fields = [(u_v, 0), (v_v, 0), (u_v, 1), (v_v, 1)]
            here = [tile(ref, level, half, g) for ref, half in fields]
            for w in range(4):
                rows = pl.ds(pl.multiple_of(16 * slot_of(4 * g + w) + 8 * level, 8), 8)
                uv_out[rows, :] = quarters(here, -32 * w)
            rim = jnp.zeros((8, 128), F32)
            for q, (ref, half) in enumerate(fields):
                west = jnp.where(lane >= 96, tile(ref, level, half, before), here[q])
                east = jnp.where(lane < 32, tile(ref, level, half, after), here[q])
                rim = jnp.where(part == 2 * q, lroll(west, 8 * q + 4), rim)
                rim = jnp.where(part == 2 * q + 1, lroll(east, 8 * q + 100), rim)
            rims.append(rim)
        kappa = [tile(k_v, level, half, g) for level in range(2) for half in range(2)]
        for w in range(4):
            slot = slot_of(4 * g + w)
            both = jnp.where(lane < 32, lroll(rims[0], -32 * w), lroll(rims[1], 32 - 32 * w))
            both = jnp.where(lane < 64, both, lroll(sroll(both, 4), 64))
            ek_out[slot, 0, :, :] = both[0:4, :]
            block = quarters(kappa, -32 * w)
            ek_out[slot, 1, :, :] = block[0:4, :]
            ek_out[slot, 2, :, :] = block[4:8, :]
        return carry

    lax.fori_loop(0, 8, group, 0)


def level_base(group):
    return (lax.rem(group, 2) * 4 + group // 2) * 128


def level_rows(group, row):
    return pl.ds(level_base(group) + row, 8, stride=16)


def pack_halos(x_v, lon_out, lat_out):
    def one(group, carry):
        for b in range(4):
            west, east = [], []
            for i in range(4):
                west.append(x_v[0, level_rows(group, 4 * b + i), :])
                east.append(x_v[1, level_rows(group, 4 * b + i), :])
                if b in (0, 3):
                    side = 0 if b == 0 else 1
                    lat_out[side, group, i, :, 0:128] = west[i]
                    lat_out[side, group, i, :, 128:256] = east[i]
            lon_out[0, b, group, :, :] = quarters(west, 0)
            lon_out[1, b, group, :, :] = quarters(east, 32)
        return carry

    lax.fori_loop(0, NG, one, 0)


def transport(group, x_v, uv_in, uv_n, uv_s, e_in, e_n, e_s, lon_h, lon_n, lon_s, lat_n, lat_s, w, out, base):
    lane, sub = iota(1), iota(0)
    column = lane // 8
    rim = jnp.where(lane < 32, 4 + column, jnp.where(lane >= 96, column - 12, 0)) + 32 * lax.rem(sub, 2)

    parts = ((uv_in, e_in, 0, 0, 8, 4), (uv_in, e_in, 1, 0, 8, 12), (uv_n, e_n, 0, 0, 4, 20), (uv_s, e_s, 1, 4, 8, 0))

    def spread(f, carry):
        for half in range(2):
            for t in range(2):
                index = column + (64 * half + 16 * t + 32 * f)
                for uv, _, h, first, end, at in parts:
                    if h == half:
                        for r in range(first, end):
                            tile = uv[pl.ds(64 * group + r, 8, stride=8), :]
                            w[f, at + r - first, t, :, :] = lanes_of(tile, index)
            for j in range(2):
                index = rim + (64 * j + 16 * half + 8 * f)
                for _, e, h, first, end, at in parts:
                    if h == half:
                        for r in range(max(first, 4 * j), min(end, 4 * j + 4)):
                            edge = e[pl.ds(32 * group + r % 4, 8, stride=4), :]
                            w[f, at + r - first, 2, :, :] = lanes_of(edge, index)
        return carry

    lax.fori_loop(0, 2, spread, 0)

    def field(row):
        if row < 0:
            tiles = [lat_s[group, row + 4, :, 128 * t : 128 * t + 128] for t in range(2)]
            east, west = lon_s[0, group, :, :], lon_s[1, group, :, :]
        elif row >= 16:
            tiles = [lat_n[group, row - 16, :, 128 * t : 128 * t + 128] for t in range(2)]
            east, west = lon_n[0, group, :, :], lon_n[1, group, :, :]
        else:
            tiles = [x_v[t, level_rows(group, row), :] for t in range(2)]
            east, west = lon_h[0, row // 4, group, :, :], lon_h[1, row // 4, group, :, :]
        q = row % 4
        side = jnp.where(lane < 32, lroll(east, -32 * q), jnp.where(lane >= 96, lroll(west, 96 - 32 * q), 0.0))
        return tiles + [side]

    stages = [dict() for _ in range(NSUB + 1)]
    below = [None] * (NSUB + 1)
    for time in range(-4, 20 + LAG * NSUB):
        if time < 20:
            stages[0][time] = field(time)
        for step in range(NSUB, 0, -1):
            row = time - LAG * step
            before = stages[step - 1]
            if row not in before or row + 1 not in before:
                continue
            lower, upper = before.pop(row), before[row + 1]
            size = 3 if step < NSUB else 2
            v = [w[1, row + 4, t, :, :] for t in range(size)]
            b = [upper[t] - lower[t] for t in range(size)]
            south = below[step]
            below[step] = [jnp.minimum(v[t], 0.0) * b[t] for t in range(size)]
            if row == step - 5:
                continue
            u = [w[0, row + 4, t, :, :] for t in range(3)]
            left = [lroll(lower[t], -8) for t in range(3)]
            a = [jnp.where(lane < 120, left[t], left[(t + 1) % 3]) - lower[t] for t in range(3)]
            h = [lroll(jnp.minimum(u[t], 0.0) * a[t], 8) for t in range(3)]
            fresh = []
            for t in range(size):
                value = lower[t] + jnp.maximum(u[t], 0.0) * a[t]
                value = value + jnp.where(lane >= 8, h[t], h[(t + 2) % 3])
                value = value + jnp.maximum(v[t], 0.0) * b[t]
                fresh.append(value + south[t])
            if step < NSUB:
                stages[step][row] = fresh
            else:
                for t in range(2):
                    out[t, pl.ds(base + row, 8, stride=16), :] = fresh[t]


def factor(k_in, f_v, r_v):
    lane = iota(1)
    low = lane < 64

    def block(m):
        return k_in[pl.ds(pl.multiple_of(8 * slot_of(m), 8), 8), :]

    a = jnp.where(low, 1.0, 1.0 + block(31))
    b = jnp.ones((8, 128), F32)

    def four(i, carry):
        a, b = carry
        for n in range(4):
            m = 4 * i + n
            here, there = block(m), block(31 - m)
            beyond = block(jnp.maximum(30 - m, 0))
            for l in range(2):
                if l == 0:
                    kappa = jnp.where(low, here, lroll(there, 64))
                else:
                    kappa = jnp.where(low, lroll(here, 64), beyond)
                last = a * b
                nexta, nextb = a + kappa * (a + b), a + kappa * b
                inv = b / nextb
                f_v[2 * m + l, :, :] = kappa * inv
                r_v[2 * m + l, :, :] = inv
                if n == 3 and l == 1:
                    p = a / b
                    other = lroll(p, 64)
                    det = 1.0 / (p * other + kappa * (p + other))

                    @pl.when(i == 3)
                    def _():
                        f_v[31, :, :] = kappa * det
                        r_v[31, :, :] = (other + kappa) * det

                a, b = nexta, nextb
        scale = 1.0 / b
        return (a * scale, jnp.ones((8, 128), F32))

    lax.fori_loop(0, 4, four, (a, b))


PLACES = [(h, t) for h in range(2) for t in range(2)]


def widen(f_v, r_v, f_w, r_w):
    column = iota(1) // 8

    def some(i, carry):
        for end in range(2):
            for n, (h, t) in enumerate(PLACES):
                index = column + (64 * end + 32 * h + 16 * t)
                for src, dst in ((f_v, f_w), (r_v, r_w)):
                    for j in range(8):
                        dst[8 * i + j, 4 * end + n, :, :] = lanes_of(src[8 * i + j, :, :], index)
        return carry

    lax.fori_loop(0, 4, some, 0)


def solve(x_v, f_w, r_w, out):
    spots = [(end, h, t) for end in range(2) for h, t in PLACES]

    def rows(j, end, h):
        level = j if end == 0 else 63 - j
        return pl.ds(pl.multiple_of(16 * level + 8 * h, 8), 8)

    def forward(i, carry):
        total, before = carry
        for n in range(4):
            j = 4 * i + n
            total = [x_v[t, rows(j, end, h), :] + f * s for (end, h, t), f, s in zip(spots, before, total)]
            before = [f_w[j, n, :, :] for n in range(8)]
            for n, (end, h, t) in enumerate(spots):
                x_v[t, rows(j, end, h), :] = r_w[j, n, :, :] * total[n]
        return (total, before)

    zeros = [jnp.zeros((8, 128), F32) for _ in spots]
    total, before = lax.fori_loop(0, 8, forward, (zeros, zeros))
    above = [r_w[31, n, :, :] * total[n] + before[n] * total[(n + 4) % 8] for n in range(8)]

    def put(j, values):
        for n, (end, h, t) in enumerate(spots):
            out[rows(j, end, h), 128 * t : 128 * t + 128] = values[n]

    put(31, above)

    def one(j, above):
        above = [x_v[t, rows(j, end, h), :] + f_w[j, n, :, :] * above[n] for n, (end, h, t) in enumerate(spots)]
        put(j, above)
        return above

    for n in range(1, 8):
        above = one(31 - n, above)

    def chunk(c, above):
        for n in range(8):
            above = one(31 - 8 * c - n, above)
        return above

    lax.fori_loop(1, 4, chunk, above)


def pack_surface(x_v, sf_v, turn, out):
    lane = lax.broadcasted_iota(jnp.int32, (32, 128), 1)
    for t in range(2):
        cols = slice(128 * t, 128 * t + 128)
        value = sf_v[:, cols] * x_v[t, 0:16, :]
        block = jnp.concatenate([value, jnp.zeros((112, 128), F32)], axis=0)
        turn[cols, :] = block.T
    total = turn[pl.ds(0, 32, stride=TRAC), :]
    for t in range(1, TRAC):
        piece = pltpu.roll(turn[pl.ds(t, 32, stride=TRAC), :], 16 * t, 1)
        total = jnp.where(jnp.logical_and(lane >= 16 * t, lane < 16 * t + 16), piece, total)
    out[...] = total


def unpack_flux(value, turn, out):
    for t in range(TRAC):
        piece = value if t == 0 else pltpu.roll(value, 128 - 16 * t, 1)
        turn[pl.ds(t, 32, stride=TRAC), :] = piece
    for t in range(2):
        cols = slice(128 * t, 128 * t + 128)
        out[:, cols] = turn[cols, :].T[:16]


def kernel(
    x_hbm, u_hbm, v_hbm, k_hbm, sf_hbm, zt_hbm, out, flux_out,
    x_v, u_v, v_v, k_v, sf_v, zt_v,
    uv_out, uv_in, uv_n, uv_s, ek_out, ek_in, e_in, e_n, e_s, k_in, f_v, r_v, f_w, r_w, w_v,
    lon_out, lon_h, lon_n, lon_s, lat_out, lat_n, lat_s, turn, ring, out_v,
    uv0_in, uv0_n, uv0_s, e0_in, e0_n, e0_s, y_v,
    in_sem, ek_ss, ek_rs, uv_ss, uv_rs, lat_ss, lat_rs, lon_ss, lon_rs,
    cor_ss, cor_rs, fwd_ss, fwd_rs, far_ss, near_ss, x_ss, ring_rs, out_sem, first_ss, first_rs,
):
    a, me = lax.axis_index("lat"), lax.axis_index("lon")
    z, x = lax.rem(me, NZ), me // NZ
    mine = slot_of(me)
    early = z < HALF
    has_n, has_s = a < NLA - 1, a > 0
    east = lax.rem(me + 1, NLO)
    west = lax.rem(me + NLO - 1, NLO)

    def tiled(ref, t):
        return ref.at[:, 128 * t : 128 * t + 128]

    pairs = ((u_hbm, u_v), (v_hbm, v_v), (k_hbm, k_v), (tiled(x_hbm, 0), x_v.at[0]), (tiled(x_hbm, 1), x_v.at[1]), (sf_hbm, sf_v), (zt_hbm, zt_v))
    loads = [pltpu.make_async_copy(src, dst, in_sem.at[i]) for i, (src, dst) in enumerate(pairs)]
    for load in loads:
        load.start()

    def each(count, action):
        def body(i, carry):
            action(i)
            return carry

        lax.fori_loop(0, count, body, 0)

    barrier = pltpu.get_barrier_semaphore()

    def nth(j):
        return lax.rem(j, 2) * NZ + j // 2

    def greet(lon):
        @pl.when(lon != me)
        def _():
            pl.semaphore_signal(barrier, inc=1, device_id=(a, lon), device_id_type=MESH)

    each(NLO // 2, lambda j: greet(nth(NLO // 2 + j)))

    each(NLO // 2, lambda j: greet(nth(j)))

    @pl.when(has_n)
    def _():
        pl.semaphore_signal(barrier, inc=1, device_id=(a + 1, me), device_id_type=MESH)

    @pl.when(has_s)
    def _():
        pl.semaphore_signal(barrier, inc=1, device_id=(a - 1, me), device_id_type=MESH)

    for load in loads[:3]:
        load.wait()
    pack_slabs(u_v, v_v, k_v, uv_out, ek_out, a == NLA - 1)
    loads[3].wait()
    loads[4].wait()
    pack_halos(x_v, lon_out, lat_out)

    uv_in[rows16(mine), :] = uv_out[rows16(mine), :]
    ek_in[mine] = ek_out[mine]

    @pl.when(jnp.logical_not(has_n))
    def _():
        for ref in (lat_n, lon_n, uv_n, e_n, uv0_n, e0_n):
            ref[...] = jnp.zeros_like(ref)

    @pl.when(jnp.logical_not(has_s))
    def _():
        for ref in (lat_s, lon_s, uv_s, e_s, uv0_s, e0_s):
            ref[...] = jnp.zeros_like(ref)

    for ref in (uv0_in, uv0_n, uv0_s):
        ref[16:64, :] = jnp.zeros((48, 128), F32)
    for ref in (e0_in, e0_n, e0_s):
        ref[8:32, :] = jnp.zeros((24, 128), F32)

    neighbours = jnp.where(has_n, 1, 0) + jnp.where(has_s, 1, 0)
    pl.semaphore_wait(barrier, NLO - 1 + neighbours)

    def remote(src, dst, ss, rs, device):
        return pltpu.make_async_remote_copy(
            src_ref=src, dst_ref=dst, send_sem=ss, recv_sem=rs, device_id=device, device_id_type=MESH
        )

    def send_ek(lon):
        s = slot_of(lon)
        return remote(ek_out.at[s], ek_in.at[mine], ek_ss.at[s], ek_rs.at[mine], (a, lon))

    def send_uv(lon):
        s = slot_of(lon)
        return remote(uv_out.at[rows16(s)], uv_in.at[rows16(mine)], uv_ss.at[s], uv_rs.at[mine], (a, lon))

    def recv_ek(slot):
        return remote(ek_out.at[slot], ek_in.at[slot], ek_ss.at[slot], ek_rs.at[slot], (a, lon_of(slot)))

    def recv_uv(slot):
        rows = rows16(slot)
        return remote(uv_out.at[rows], uv_in.at[rows], uv_ss.at[slot], uv_rs.at[slot], (a, lon_of(slot)))

    def span(c):
        return pl.ds(c * PER, PER)

    def lat_north(c):
        return remote(lat_out.at[1, span(c)], lat_s.at[span(c)], lat_ss.at[1, c], lat_rs.at[1, c], (a + 1, me))

    def lat_south(c):
        return remote(lat_out.at[0, span(c)], lat_n.at[span(c)], lat_ss.at[0, c], lat_rs.at[0, c], (a - 1, me))

    def lon_west(c):
        return remote(lon_out.at[0, :, span(c)], lon_h.at[0, :, span(c)], lon_ss.at[0, c], lon_rs.at[0, c], (a, west))

    def lon_east(c):
        return remote(lon_out.at[1, :, span(c)], lon_h.at[1, :, span(c)], lon_ss.at[1, c], lon_rs.at[1, c], (a, east))

    def cor_north(side, c):
        ref, dst = lon_h.at[side, 3, span(c)], lon_s.at[side, span(c)]
        return remote(ref, dst, cor_ss.at[1, side, c], cor_rs.at[1, side, c], (a + 1, me))

    def cor_south(side, c):
        ref, dst = lon_h.at[side, 0, span(c)], lon_n.at[side, span(c)]
        return remote(ref, dst, cor_ss.at[0, side, c], cor_rs.at[0, side, c], (a - 1, me))

    def uv_rows(group):
        return pl.ds(pl.multiple_of(64 * group, 64), 64)

    def e_rows(group):
        return pl.ds(pl.multiple_of(32 * group, 32), 32)

    def fwd_north(group):
        r, e = uv_rows(group), e_rows(group)
        return (
            remote(uv_in.at[r], uv_s.at[r], fwd_ss.at[1, 0, group], fwd_rs.at[1, 0, group], (a + 1, me)),
            remote(e_in.at[e], e_s.at[e], fwd_ss.at[1, 1, group], fwd_rs.at[1, 1, group], (a + 1, me)),
        )

    def fwd_south(group):
        r, e = uv_rows(group), e_rows(group)
        return (
            remote(uv_in.at[r], uv_n.at[r], fwd_ss.at[0, 0, group], fwd_rs.at[0, 0, group], (a - 1, me)),
            remote(e_in.at[e], e_n.at[e], fwd_ss.at[0, 1, group], fwd_rs.at[0, 1, group], (a - 1, me)),
        )

    def spread_blocks(order, first, count):
        def one(i):
            lon = lax.rem(first + i, 2) * NZ + order(first + i)

            @pl.when(lon != me)
            def _():
                send_ek(lon).start()
                send_uv(lon).start()

        each(count, one)

    def send_halos(first, count):
        def one(i):
            lon_east(first + i).start()
            lon_west(first + i).start()

            @pl.when(has_n)
            def _():
                lat_north(first + i).start()

            @pl.when(has_s)
            def _():
                lat_south(first + i).start()

        each(count, one)

    def place_at(j):
        return jnp.where(me == 0, NZ - 1 - j // 2, j // 2)

    send_halos(0, 1)
    spread_blocks(place_at, 0, NLO // 4)
    send_halos(1, CH - 1)
    spread_blocks(place_at, NLO // 4, NLO - NLO // 4)

    loads[5].wait()
    loads[6].wait()

    def corners(c):
        lon_west(c).wait_recv()
        lon_east(c).wait_recv()

        @pl.when(has_n)
        def _():
            cor_north(0, c).start()
            cor_north(1, c).start()

        @pl.when(has_s)
        def _():
            cor_south(0, c).start()
            cor_south(1, c).start()

    def halos_here(c):
        @pl.when(has_n)
        def _():
            lat_south(c).wait_recv()
            cor_south(0, c).wait_recv()
            cor_south(1, c).wait_recv()

        @pl.when(has_s)
        def _():
            lat_north(c).wait_recv()
            cor_north(0, c).wait_recv()
            cor_north(1, c).wait_recv()

    def first_north():
        return (
            remote(uv0_in.at[0:16], uv0_s.at[0:16], first_ss.at[1, 0], first_rs.at[1, 0], (a + 1, me)),
            remote(e0_in.at[0:8], e0_s.at[0:8], first_ss.at[1, 1], first_rs.at[1, 1], (a + 1, me)),
        )

    def first_south():
        return (
            remote(uv0_in.at[0:16], uv0_n.at[0:16], first_ss.at[0, 0], first_rs.at[0, 0], (a - 1, me)),
            remote(e0_in.at[0:8], e0_n.at[0:8], first_ss.at[0, 1], first_rs.at[0, 1], (a - 1, me)),
        )

    corners(0)

    @pl.when(me != 0)
    def _():
        recv_ek(0).wait_recv()
        recv_uv(0).wait_recv()

    uv0_in[0:16, :] = uv_in[0:16, :]
    e0_in[0:8, :] = jnp.concatenate([ek_in[0, 0, :, :], ek_in[0, 0, :, :]], axis=0)

    @pl.when(has_n)
    def _():
        for copy in first_north():
            copy.start()

    @pl.when(has_s)
    def _():
        for copy in first_south():
            copy.start()

    each(CH - 1, lambda c: corners(c + 1))

    def pass_on(group):
        def one(i):
            slot = 4 * group + i

            @pl.when(jnp.logical_and(slot != mine, slot != 0))
            def _():
                recv_ek(slot).wait_recv()
                recv_uv(slot).wait_recv()

            rims = ek_in[slot, 0, :, :]
            at = pl.multiple_of(8 * slot, 8)
            e_in[pl.ds(at, 8), :] = jnp.concatenate([rims, rims], axis=0)
            k_in[pl.ds(at, 8), :] = jnp.concatenate([ek_in[slot, 1, :, :], ek_in[slot, 2, :, :]], axis=0)

        each(4, one)

        @pl.when(has_n)
        def _():
            for copy in fwd_north(group):
                copy.start()

        @pl.when(has_s)
        def _():
            for copy in fwd_south(group):
                copy.start()

    over = (1 - x) * NZ + z

    def place(d):
        return lax.rem(z + d, NZ)

    FAR, NEAR = (4, 12, 8), (1, 15, 2)

    def ring_send(block, device, sem):
        return remote(ring.at[block], ring.at[block], sem, ring_rs.at[block], (a, device))

    def ring_far(i):
        return ring_send(me, x * NZ + place(FAR[i]), far_ss.at[i])

    def ring_near(k, i):
        block = x * NZ + place((0, 4, 12, 8)[k])
        return ring_send(block, x * NZ + place(NEAR[i]), near_ss.at[k, i])

    def ring_over(d):
        zz = place(d)
        return ring_send(x * NZ + zz, over, x_ss.at[zz])

    def ring_recv(block):
        return ring_send(block, over, x_ss.at[0])

    def ring_start():
        pack_surface(y_v, sf_v, turn, ring.at[me])
        for i in range(3):
            ring_far(i).start()
        ring_over(0).start()
        for i in range(3):
            ring_near(0, i).start()

    def ring_middle():
        for k, d in enumerate((4, 12, 8)):
            ring_recv(x * NZ + place(d)).wait_recv()
            for i in range(3):
                ring_near(k + 1, i).start()
            ring_over(d).start()

    def ring_end():
        for d in range(NZ):
            if d % 4:
                ring_recv(x * NZ + place(d)).wait_recv()
                ring_over(d).start()

    halos_here(0)

    @pl.when(has_n)
    def _():
        for copy in first_south():
            copy.wait_recv()

    @pl.when(has_s)
    def _():
        for copy in first_north():
            copy.wait_recv()

    transport(0, x_v, uv0_in, uv0_n, uv0_s, e0_in, e0_n, e0_s, lon_h, lon_n, lon_s, lat_n, lat_s, w_v, y_v, 0)
    ring_start()
    ring_middle()
    each(LOOK, pass_on)

    def turn_of(group):
        @pl.when(group + LOOK < NG)
        def _():
            pass_on(group + LOOK)

        @pl.when(jnp.logical_and(lax.rem(group, PER) == 0, group > 0))
        def _():
            halos_here(group // PER)

        @pl.when(has_n)
        def _():
            for copy in fwd_south(group):
                copy.wait_recv()

        @pl.when(has_s)
        def _():
            for copy in fwd_north(group):
                copy.wait_recv()

        transport(
            group, x_v, uv_in, uv_n, uv_s, e_in, e_n, e_s, lon_h, lon_n, lon_s, lat_n, lat_s, w_v, x_v, level_base(group)
        )

        @pl.when(group == 1)
        def _():
            ring_end()

        @pl.when(group == NG - 2)
        def _():
            factor(k_in, f_v, r_v)
            widen(f_v, r_v, f_w, r_w)

    each(NG, turn_of)

    def store(c):
        rows = pl.ds(256 * c, 256)
        return pltpu.make_async_copy(out_v.at[rows], out.at[rows], out_sem.at[c])

    solve(x_v, f_w, r_w, out_v)
    for c in range(4):
        store(c).start()

    each(NZ, lambda zz: ring_recv((1 - x) * NZ + zz).wait_recv())
    gathered = ring[...].reshape(NLO * 32, 128)
    turned = jnp.dot(zt_v[...], gathered, precision=lax.Precision.HIGHEST, preferred_element_type=F32)
    unpack_flux(turned, turn, flux_out)

    def sent(lon):
        @pl.when(lon != me)
        def _():
            send_ek(lon).wait_send()
            send_uv(lon).wait_send()

    each(NLO, sent)
    for c in range(4):
        store(c).wait()

    def sent_group(group):
        @pl.when(has_n)
        def _():
            for copy in fwd_north(group):
                copy.wait_send()

        @pl.when(has_s)
        def _():
            for copy in fwd_south(group):
                copy.wait_send()

    each(NG, sent_group)

    @pl.when(has_n)
    def _():
        for copy in first_north():
            copy.wait_send()

    @pl.when(has_s)
    def _():
        for copy in first_south():
            copy.wait_send()

    def sent_chunk(c):
        lon_east(c).wait_send()
        lon_west(c).wait_send()

        @pl.when(has_n)
        def _():
            lat_north(c).wait_send()
            cor_north(0, c).wait_send()
            cor_north(1, c).wait_send()

        @pl.when(has_s)
        def _():
            lat_south(c).wait_send()
            cor_south(0, c).wait_send()
            cor_south(1, c).wait_send()

    each(CH, sent_chunk)
    for i in range(3):
        ring_far(i).wait_send()
        for k in range(4):
            ring_near(k, i).wait_send()
    each(NZ, lambda d: ring_over(d).wait_send())


def on_device(adjoint_in, u_courant, v_courant, diffusivity, surface_factor, zonal_sqrt):
    def vmem(*shape):
        return pltpu.VMEM(shape, F32)

    def dma(*shape):
        return pltpu.SemaphoreType.DMA(shape)

    solved, flux = pl.pallas_call(
        kernel,
        name="adjoint_hour",
        out_shape=(
            jax.ShapeDtypeStruct((1024, 256), F32),
            jax.ShapeDtypeStruct(surface_factor.shape, F32),
        ),
        in_specs=[pl.BlockSpec(memory_space=pltpu.HBM)] * 6,
        out_specs=(pl.BlockSpec(memory_space=pl.ANY), pl.BlockSpec(memory_space=pltpu.VMEM)),
        scratch_shapes=[
            vmem(2, 1024, 128), vmem(2, 16, 1024), vmem(2, 16, 1024), vmem(2, 16, 1024),
            vmem(16, 256), vmem(32, 1024),
            vmem(512, 128), vmem(512, 128), vmem(512, 128), vmem(512, 128),
            vmem(32, 3, 4, 128), vmem(32, 3, 4, 128), vmem(256, 128), vmem(256, 128), vmem(256, 128), vmem(256, 128),
            vmem(32, 8, 128), vmem(32, 8, 128), vmem(32, 8, 8, 128), vmem(32, 8, 8, 128), vmem(2, 24, 3, 8, 128),
            vmem(2, 4, 8, 8, 128), vmem(2, 4, 8, 8, 128), vmem(2, 8, 8, 128), vmem(2, 8, 8, 128),
            vmem(2, 8, 4, 8, 256), vmem(8, 4, 8, 256), vmem(8, 4, 8, 256), vmem(256, 128), vmem(32, 32, 128), vmem(1024, 256),
            vmem(64, 128), vmem(64, 128), vmem(64, 128), vmem(32, 128), vmem(32, 128), vmem(32, 128), vmem(2, 128, 128),
            dma(7), dma(32), dma(32), dma(32), dma(32), dma(2, CH), dma(2, CH), dma(2, CH), dma(2, CH),
            dma(2, 2, CH), dma(2, 2, CH), dma(2, 2, NG), dma(2, 2, NG), dma(3), dma(4, 3), dma(16), dma(32), dma(4), dma(2, 2), dma(2, 2),
        ],
        compiler_params=pltpu.CompilerParams(
            collective_id=0, has_side_effects=True, vmem_limit_bytes=56 * 2**20
        ),
        cost_estimate=pl.CostEstimate(flops=60_000_000, bytes_accessed=3_000_000, transcendentals=0),
    )(adjoint_in.reshape(1024, 256), u_courant, v_courant, diffusivity, surface_factor, zonal_sqrt.T)
    return solved.reshape(adjoint_in.shape), flux


def solution(mesh):
    placed = (
        P(None, "lat", "lon"),
        P("lon", "lat", None),
        P("lon", "lat", None),
        P("lon", "lat", None),
        P("lat", "lon"),
        P(None, "lon"),
    )
    return jax.shard_map(
        on_device,
        mesh=mesh,
        in_specs=placed,
        out_specs=(P(None, "lat", "lon"), P("lat", "lon")),
        check_vma=False,
    )
```

profile of v0, /device:TPU:6, one launch (start us, length us, event | category | flops | bytes accessed | tf_op | source)
XLA Modules:
  0.0 73.9 jit_solution(4840588114675899847)
XLA Ops:
  0.6 70.3 %adjoint_hour.1 = (f32[1024,256]{1,0:T(8,128)}, f32[16,256]{1,0:T(8,128)}) custom-call(f32[1024,256]{1,0:T(8,128)} %bitcast.3, f32[2,16,1024]{2,1,0:T(8,128)} %u_hbm.1, f32[2,16,1024]{2,1,0:T(8,128)} %v_hbm.1, f32[2,16,1024]{2,1,0:T(8,128)} %k_hbm.1, f32[16,256]{1,0:T(8,128)} %sf_hbm.1, f32[32,1024]{1,0:T(8,128)} %bitcast.5), custom_call_target="tpu_custom_call" | custom-call | flops 60000000 | bytes 3000000 | tf_op jit(solution)/shard_map/adjoint_hour/pallas_call | solution.py:774
  71.0 0.0 copy-start
  71.0 2.3 %copy.10 = f32[64,16,256]{2,1,0:T(8,128)} copy(f32[64,16,256]{2,1,0:T(8,128)} %bitcast.4) | data formatting | bytes 2097152
  73.2 0.0 copy-done
  73.3 0.6 copy.11
Async XLA Ops:
  71.0 2.3 %copy-start = (f32[16,256]{1,0:T(8,128)S(1)}, f32[16,256]{1,0:T(8,128)}, u32[]{:S(2)}) copy-start(f32[16,256]{1,0:T(8,128)} %get-tuple-element.9) | copy-start | bytes 49156
where the time goes:
time: 74 us; the launch traced here: 73.9 us
  Pallas kernels  70.3 us (95%)
  local copies, waits for them, and re-layouts  2.88 us (4%)
    pallas_call x1, Pallas kernels, on_device(): pl.pallas_call(kernel, name='adjoint_hour', out_shape=(jax.ShapeDtypeStru...  70.3 us
    unnamed x4, local copies, waits for them, and re-layouts  2.88 us

commit v1 on v0

--- a/solution.py
+++ b/solution.py
@@ -334,9 +334,9 @@
     x_v, u_v, v_v, k_v, sf_v, zt_v,
     uv_out, uv_in, uv_n, uv_s, ek_out, ek_in, e_in, e_n, e_s, k_in, f_v, r_v, f_w, r_w, w_v,
     lon_out, lon_h, lon_n, lon_s, lat_out, lat_n, lat_s, turn, ring, out_v,
-    uv0_in, uv0_n, uv0_s, e0_in, e0_n, e0_s, y_v,
+    uv0_in, uv0_n, uv0_s, e0_in, e0_n, e0_s, y_v, zt_p, part_out, part_in, part_own,
     in_sem, ek_ss, ek_rs, uv_ss, uv_rs, lat_ss, lat_rs, lon_ss, lon_rs,
-    cor_ss, cor_rs, fwd_ss, fwd_rs, far_ss, near_ss, x_ss, ring_rs, out_sem, first_ss, first_rs,
+    cor_ss, cor_rs, fwd_ss, fwd_rs, far_ss, near_ss, part_ss, part_rs, ring_rs, out_sem, first_ss, first_rs,
 ):
     a, me = lax.axis_index("lat"), lax.axis_index("lon")
     z, x = lax.rem(me, NZ), me // NZ
@@ -500,16 +500,34 @@
 
         each(count, one)
 
-    def place_at(j):
-        return jnp.where(me == 0, NZ - 1 - j // 2, j // 2)
+    def along_z(j):
+        return j // 2
 
     send_halos(0, 1)
-    spread_blocks(place_at, 0, NLO // 4)
+
+    @pl.when(me == 0)
+    def _():
+        spread_blocks(lambda j: jnp.where(lax.rem(j // 2, 2) == 0, NZ - 1 - j // 4, j // 4), 0, NLO)
+
+    @pl.when(me != 0)
+    def _():
+        spread_blocks(along_z, 0, NLO // 4)
+
     send_halos(1, CH - 1)
-    spread_blocks(place_at, NLO // 4, NLO - NLO // 4)
+
+    @pl.when(me != 0)
+    def _():
+        spread_blocks(along_z, NLO // 4, NLO - NLO // 4)
+
+    over = (1 - x) * NZ + z
+
+    def zt_over():
+        cols = pl.ds(pl.multiple_of((1 - x) * 512, 512), 512)
+        return remote(zt_v.at[:, cols], zt_p, part_ss.at[0], part_rs.at[0], (a, over))
 
     loads[5].wait()
     loads[6].wait()
+    zt_over().start()
 
     def corners(c):
         lon_west(c).wait_recv()
@@ -570,7 +588,14 @@
         for copy in first_south():
             copy.start()
 
-    each(CH - 1, lambda c: corners(c + 1))
+
+    block = z // 4
+    step = jnp.where(lax.rem(z, 4) < 2, 3, 1)
+
+    def nth_group(i):
+        k = i // 2
+        shift = jnp.where(k == 0, 0, jnp.where(k == 1, step, jnp.where(k == 2, 4 - step, 2)))
+        return 2 * lax.rem(block + shift, 4) + lax.rem(x + i, 2)
 
     def pass_on(group):
         def one(i):
@@ -598,50 +623,59 @@
             for copy in fwd_south(group):
                 copy.start()
 
-    over = (1 - x) * NZ + z
 
     def place(d):
         return lax.rem(z + d, NZ)
 
-    FAR, NEAR = (4, 12, 8), (1, 15, 2)
+    place_in = lax.rem(z, 4)
+    beyond = 4 * lax.rem(z // 4 + 2, 4)
+    sent_beyond, from_beyond = beyond + lax.rem(place_in + 3, 4), beyond + lax.rem(place_in + 1, 4)
+    far_to = (place(4), place(12), sent_beyond)
+    held = (z, place(4), place(12), from_beyond)
 
     def ring_send(block, device, sem):
         return remote(ring.at[block], ring.at[block], sem, ring_rs.at[block], (a, device))
 
     def ring_far(i):
-        return ring_send(me, x * NZ + place(FAR[i]), far_ss.at[i])
+        return ring_send(me, x * NZ + far_to[i], far_ss.at[i])
 
     def ring_near(k, i):
-        block = x * NZ + place((0, 4, 12, 8)[k])
-        return ring_send(block, x * NZ + place(NEAR[i]), near_ss.at[k, i])
-
-    def ring_over(d):
-        zz = place(d)
-        return ring_send(x * NZ + zz, over, x_ss.at[zz])
+        block = x * NZ + held[k]
+        return ring_send(block, x * NZ + 4 * (z // 4) + lax.rem(z + 1 + i, 4), near_ss.at[k, i])
 
     def ring_recv(block):
-        return ring_send(block, over, x_ss.at[0])
+        return ring_send(block, over, part_ss.at[0])
+
+    def part_over():
+        return remote(part_out, part_in, part_ss.at[1], part_rs.at[1], (a, over))
 
     def ring_start():
         pack_surface(y_v, sf_v, turn, ring.at[me])
         for i in range(3):
             ring_far(i).start()
-        ring_over(0).start()
         for i in range(3):
             ring_near(0, i).start()
 
     def ring_middle():
-        for k, d in enumerate((4, 12, 8)):
-            ring_recv(x * NZ + place(d)).wait_recv()
+        for k in range(1, 4):
+            ring_recv(x * NZ + held[k]).wait_recv()
             for i in range(3):
-                ring_near(k + 1, i).start()
-            ring_over(d).start()
+                ring_near(k, i).start()
 
     def ring_end():
-        for d in range(NZ):
-            if d % 4:
-                ring_recv(x * NZ + place(d)).wait_recv()
-                ring_over(d).start()
+        for d in range(1, NZ):
+            if d not in (4, 12):
+
+                @pl.when(place(d) != from_beyond)
+                def _():
+                    ring_recv(x * NZ + place(d)).wait_recv()
+
+        gathered = ring[pl.ds(x * NZ, NZ)].reshape(NZ * 32, 128)
+        zt_over().wait_recv()
+        part_out[...] = jnp.dot(zt_p[...], gathered, precision=lax.Precision.HIGHEST, preferred_element_type=F32)
+        part_over().start()
+        own = zt_v[:, pl.ds(pl.multiple_of(x * 512, 512), 512)]
+        part_own[...] = jnp.dot(own, gathered, precision=lax.Precision.HIGHEST, preferred_element_type=F32)
 
     halos_here(0)
 
@@ -657,15 +691,18 @@
 
     transport(0, x_v, uv0_in, uv0_n, uv0_s, e0_in, e0_n, e0_s, lon_h, lon_n, lon_s, lat_n, lat_s, w_v, y_v, 0)
     ring_start()
+    each(CH - 1, lambda c: corners(c + 1))
     ring_middle()
-    each(LOOK, pass_on)
-
-    def turn_of(group):
-        @pl.when(group + LOOK < NG)
-        def _():
-            pass_on(group + LOOK)
-
-        @pl.when(jnp.logical_and(lax.rem(group, PER) == 0, group > 0))
+    each(LOOK, lambda i: pass_on(nth_group(i)))
+
+    def turn_of(i):
+        group = nth_group(i)
+
+        @pl.when(i + LOOK < NG)
+        def _():
+            pass_on(nth_group(i + LOOK))
+
+        @pl.when(jnp.logical_and(lax.rem(i, PER) == 0, group // PER > 0))
         def _():
             halos_here(group // PER)
 
@@ -683,11 +720,11 @@
             group, x_v, uv_in, uv_n, uv_s, e_in, e_n, e_s, lon_h, lon_n, lon_s, lat_n, lat_s, w_v, x_v, level_base(group)
         )
 
-        @pl.when(group == 1)
+        @pl.when(i == 1)
         def _():
             ring_end()
 
-        @pl.when(group == NG - 2)
+        @pl.when(i == NG - LOOK)
         def _():
             factor(k_in, f_v, r_v)
             widen(f_v, r_v, f_w, r_w)
@@ -702,10 +739,8 @@
     for c in range(4):
         store(c).start()
 
-    each(NZ, lambda zz: ring_recv((1 - x) * NZ + zz).wait_recv())
-    gathered = ring[...].reshape(NLO * 32, 128)
-    turned = jnp.dot(zt_v[...], gathered, precision=lax.Precision.HIGHEST, preferred_element_type=F32)
-    unpack_flux(turned, turn, flux_out)
+    part_over().wait_recv()
+    unpack_flux(part_own[...] + part_in[...], turn, flux_out)
 
     def sent(lon):
         @pl.when(lon != me)
@@ -761,7 +796,8 @@
         ring_far(i).wait_send()
         for k in range(4):
             ring_near(k, i).wait_send()
-    each(NZ, lambda d: ring_over(d).wait_send())
+    zt_over().wait_send()
+    part_over().wait_send()
 
 
 def on_device(adjoint_in, u_courant, v_courant, diffusivity, surface_factor, zonal_sqrt):
@@ -789,8 +825,9 @@
             vmem(2, 4, 8, 8, 128), vmem(2, 4, 8, 8, 128), vmem(2, 8, 8, 128), vmem(2, 8, 8, 128),
             vmem(2, 8, 4, 8, 256), vmem(8, 4, 8, 256), vmem(8, 4, 8, 256), vmem(256, 128), vmem(32, 32, 128), vmem(1024, 256),
             vmem(64, 128), vmem(64, 128), vmem(64, 128), vmem(32, 128), vmem(32, 128), vmem(32, 128), vmem(2, 128, 128),
+            vmem(32, 512), vmem(32, 128), vmem(32, 128), vmem(32, 128),
             dma(7), dma(32), dma(32), dma(32), dma(32), dma(2, CH), dma(2, CH), dma(2, CH), dma(2, CH),
-            dma(2, 2, CH), dma(2, 2, CH), dma(2, 2, NG), dma(2, 2, NG), dma(3), dma(4, 3), dma(16), dma(32), dma(4), dma(2, 2), dma(2, 2),
+            dma(2, 2, CH), dma(2, 2, CH), dma(2, 2, NG), dma(2, 2, NG), dma(3), dma(4, 3), dma(2), dma(2), dma(32), dma(4), dma(2, 2), dma(2, 2),
         ],
         compiler_params=pltpu.CompilerParams(
             collective_id=0, has_side_effects=True, vmem_limit_bytes=56 * 2**20

time: 74 us -> 72 us (0.973)
  the two profiles are of different devices: /device:TPU:6 before, /device:TPU:102 now
where the time goes in v1:
time: 72 us; the launch traced here: 71.8 us
  Pallas kernels  68.3 us (95%)
  local copies, waits for them, and re-layouts  2.88 us (4%)
    pallas_call x1, Pallas kernels, on_device(): pl.pallas_call(kernel, name='adjoint_hour', out_shape=(jax.ShapeDtypeStru...  68.3 us
    unnamed x4, local copies, waits for them, and re-layouts  2.88 us

profile of v1, /device:TPU:102, one launch (start us, length us, event | category | flops | bytes accessed | tf_op | source)
XLA Modules:
  0.0 71.8 jit_solution(6184525033839449050)
XLA Ops:
  0.6 68.3 %adjoint_hour.1 = (f32[1024,256]{1,0:T(8,128)}, f32[16,256]{1,0:T(8,128)}) custom-call(f32[1024,256]{1,0:T(8,128)} %bitcast.3, f32[2,16,1024]{2,1,0:T(8,128)} %u_hbm.1, f32[2,16,1024]{2,1,0:T(8,128)} %v_hbm.1, f32[2,16,1024]{2,1,0:T(8,128)} %k_hbm.1, f32[16,256]{1,0:T(8,128)} %sf_hbm.1, f32[32,1024]{1,0:T(8,128)} %bitcast.5), custom_call_target="tpu_custom_call" | custom-call | flops 60000000 | bytes 3000000 | tf_op jit(solution)/shard_map/adjoint_hour/pallas_call | solution.py:810
  68.9 0.0 copy-start
  69.0 2.3 %copy.10 = f32[64,16,256]{2,1,0:T(8,128)} copy(f32[64,16,256]{2,1,0:T(8,128)} %bitcast.4) | data formatting | bytes 2097152
  71.2 0.0 copy-done
  71.2 0.6 copy.11
Async XLA Ops:
  68.9 2.3 %copy-start = (f32[16,256]{1,0:T(8,128)S(1)}, f32[16,256]{1,0:T(8,128)}, u32[]{:S(2)}) copy-start(f32[16,256]{1,0:T(8,128)} %get-tuple-element.9) | copy-start | bytes 49156
